TPU v7x, 32 devices: a whole 2x2x4 slice. The times are simulated.
32 devices in a mesh: dom: 16 (over z, x, core), rep: 2 (over y).
Axes of the slice: x: 2, y: 2, z: 4, core: 2. Of those that a mesh axis runs over, the one named last changes fastest.
Arguments:
- date_key: int32 [4096, 128], P('dom'), may hold values from 0 to 1791
- item_key: int32 [4096, 128], P('dom'), may hold values from 0 to 229375
- store_key: int32 [4096, 128], P('dom'), may hold values from 0 to 127
- measures: float32 [4096, 4, 128], P('dom'), may hold values from 0 to 2
- block_count: int32 [16], P('dom'), may hold values from 1 to 256, 1664 in all
- item_price: float32 [229376], P(('dom', 'rep')), may hold values from 0 to 1
- store_region: int32 [128], replicated, may hold values from 0 to 31
- date_flag: int32 [1792], replicated, may hold values 0 or 1
Outputs:
- region_profit: float32 [3, 32, 256], P(None, None, 'rep')
Inputs may be any that keep to these rules, and one draw needn't show every extreme that they name: `block_count`: the live blocks of an index of dom are the first of its slots; the counts sum to 1664 and one index holds 256.
All inputs are finite; a program needn't handle non-finite values.
Results may differ from a plain program's by a relative error of at most 0.0028.
Values may be sent and summed in bfloat16 or wider, within the bound.
A program may use at most 64 MiB of HBM per device.

v0:
```python
import jax
import jax.numpy as jnp
from jax import lax
from jax.sharding import PartitionSpec as P

AGGS = 3
REG_DEV = 2
WEEKS = 256


low_price = 0.2
high_price = 0.8
week_length = 7


def aggregate(measures, passing):
    quantity = measures[:, 0]
    selling = measures[:, 1]
    wholesale = measures[:, 2]
    coupon = measures[:, 3]
    profit = quantity * (selling - wholesale) - coupon
    revenue = quantity * selling - coupon
    stacked = jnp.stack([profit, revenue, quantity], axis=1)
    return (stacked * passing[:, None, :]).astype(jnp.bfloat16)


def pick_half(source, member, shares):
    shaped = source.reshape((source.shape[0] // shares, shares) + source.shape[1:])
    return lax.dynamic_index_in_dim(shaped, member, axis=1, keepdims=False)


def group_sums(totals, values, group_keys, live_slots, region_count, week_first):
    slot_total, block_rows = group_keys.shape
    per_step = min(slot_total, max(1, 2048 // block_rows))
    step_rows = per_step * block_rows
    column_count = totals.shape[1]

    def add_step(step_index, running):
        first_slot = step_index * per_step
        value_part = lax.dynamic_slice_in_dim(values, first_slot, per_step, 0)
        key_part = lax.dynamic_slice_in_dim(group_keys, first_slot, per_step, 0).reshape(step_rows)
        flat_values = jnp.transpose(value_part, (1, 0, 2)).reshape(AGGS, step_rows)
        region_row = key_part // WEEKS
        week_row = key_part % WEEKS - week_first
        region_hot = (
            lax.broadcasted_iota(jnp.int32, (region_count, step_rows), 0) == region_row[None, :]
        ).astype(jnp.bfloat16)
        left_side = (flat_values[:, None, :] * region_hot[None, :, :]).reshape(
            AGGS * region_count, step_rows
        )
        week_hot = (
            lax.broadcasted_iota(jnp.int32, (step_rows, column_count), 1) == week_row[:, None]
        ).astype(jnp.bfloat16)
        return running + jnp.dot(left_side, week_hot, preferred_element_type=jnp.float32)

    step_count = (live_slots + per_step - 1) // per_step
    return lax.fori_loop(0, step_count, add_step, totals)


def per_device(
    date_key, item_key, store_key, measures, block_count, item_price, store_region, date_flag
):
    dom_size = lax.axis_size("dom")
    rep_size = lax.axis_size("rep")
    rep_index = lax.axis_index("rep")
    region_count = REG_DEV * dom_size
    half_weeks = WEEKS // rep_size
    resident = block_count[0]
    date_key = pick_half(date_key, rep_index, rep_size)
    item_key = pick_half(item_key, rep_index, rep_size)
    store_key = pick_half(store_key, rep_index, rep_size)
    measures = pick_half(measures, rep_index, rep_size)
    resident = jnp.maximum(resident - rep_index + rep_size - 1, 0) // rep_size
    week_first = 0
    column_count = WEEKS
    slot_total, block_rows = date_key.shape
    prices = lax.all_gather(item_price, ("dom", "rep"), axis=0, tiled=True)
    price_row = jnp.take(prices, item_key)
    item_ok = ((price_row >= low_price) & (price_row <= high_price)).astype(jnp.int32)
    slot_live = lax.broadcasted_iota(jnp.int32, (slot_total,), 0) < resident
    day_ok = jnp.take(date_flag, date_key)
    passing = (slot_live[:, None] & (item_ok == 1) & (day_ok == 1)).astype(jnp.float32)
    values = aggregate(measures, passing)
    group_keys = jnp.take(store_region, store_key) * WEEKS + date_key // week_length
    totals = jnp.zeros((AGGS * region_count, column_count), jnp.float32)
    totals = group_sums(totals, values, group_keys, resident, region_count, week_first)
    totals = lax.psum_scatter(
        totals.astype(jnp.bfloat16), "rep", scatter_dimension=1, tiled=True
    ).astype(jnp.float32)
    totals = lax.psum(totals, "dom")
    return totals.reshape(AGGS, region_count, half_weeks)


def solution(mesh):
    placed = (
        P("dom", None),
        P("dom", None),
        P("dom", None),
        P("dom", None, None),
        P("dom"),
        P(("dom", "rep")),
        P(),
        P(),
    )
    return jax.shard_map(
        per_device, mesh=mesh, in_specs=placed, out_specs=P(None, None, "rep"), check_vma=False
    )
```

profile of v0, /device:TPU:0, one launch (start us, length us, event | category | flops | bytes accessed | tf_op | source)
XLA Modules:
  0.0 446.7 jit_solution(11326210312734976980)
XLA Ops:
  6.5 0.0 copy-start
  6.5 0.0 reduce-scatter.4.cloned.1.call-start
  7.3 1.3 compare_and_fusion
  8.6 0.2 broadcast_divide_fusion
  8.8 1.0 constant_dynamic-slice_fusion.2
  9.8 0.0 copy-start.4
  9.8 0.0 copy-start.2
  9.8 75.0 %all_gather.3 = f32[229376]{0:T(1024)S(1)} all-gather(f32[7168]{0:T(1024)} %param.15), channel_id=1, replica_groups=mesh['dom'=16,'rep'=2] {'dom','rep'}, dimensions={0}, use_global_device_ids=true | all-gather | bytes 946176 | tf_op jit(solution)/shard_map/all_gather | solution.py:77
  84.9 0.0 copy-done
  84.9 0.2 fusion.15
  85.2 0.1 constant_dynamic-slice_fusion
  85.3 90.5 %gather_fusion.1 = s32[16384]{0:T(1024)S(1)} fusion(s32[1792]{0:T(1024)S(1)} %copy-done.2, s32[16384]{0:T(1024)S(1)} %fusion.11), kind=kCustom, calls=%fused_computation.1 | custom fusion | bytes 196608 | tf_op jit(solution)/shard_map/jit(_take)/gather | solution.py:81
  175.8 90.5 %gather_fusion = f32[16384]{0:T(1024)S(1)} fusion(f32[229376]{0:T(1024)S(1)} %all_gather.3, s32[16384]{0:T(1024)S(1)} %fusion.9), kind=kCustom, calls=%fused_computation | custom fusion | bytes 196608 | tf_op jit(solution)/shard_map/jit(_take)/gather | solution.py:78
  266.4 0.0 copy-start.1
  266.4 0.6 copy-done.1
  267.0 97.2 %gather_fusion.2 = s32[16384]{0:T(1024)S(1)} fusion(s32[128]{0:T(128)S(1)} %copy-done.1, s32[16384]{0:T(1024)S(1)} %fusion.13), kind=kCustom, calls=%fused_computation.2 | custom fusion | bytes 196608 | tf_op jit(solution)/shard_map/jit(_take)/gather | solution.py:84
  364.2 0.4 and_convert_fusion
  364.7 0.2 fusion.6
  365.0 6.0 %while.12 = (s32[]{:T(128)}, f32[96,256]{1,0:T(8,128)S(1)}, s32[]{:T(128)}, bf16[128,3,128]{2,1,0:T(4,128)(2,1)S(1)}, s32[128,128]{1,0:T(8,128)S(1)}, /*index=5*/s32[]{:T(128)}, s32[]{:T(128)}, s32[]{:T(128)}, s32[]{:T(128)}) while((s32[]{:T(128)}, f32[96,256]{1,0:T(8,128)S(1)}, s32[]{:T(128)}, bf16[128,3,128]{2,1,0:T(4,128)(2,1)S(1)}, ...), condition=%wide.region_1.2_spmd, body=%wide.region_0.1_spmd.sunk | while | flops 101591048 | bytes 1335447 | solution.py:57
  365.1 0.6 fusion.23
  365.9 0.6 fusion.23
  366.6 0.6 fusion.23
  367.4 0.6 fusion.23
  368.1 0.6 fusion.23
  368.9 0.6 fusion.23
  369.6 0.6 fusion.23
  370.4 0.6 fusion.23
  371.0 0.7 copy.27
  371.7 0.0 reduce-scatter.4.cloned.1.call-update
  371.7 5.9 %reduce-scatter.4.cloned.1.call-done = bf16[128,96]{1,0:T(8,128)(2,1)} async-done(((bf16[256,96]{1,0:T(8,128)(2,1)}), bf16[128,96]{1,0:T(8,128)(2,1)}) %reduce-scatter.4.cloned.1.call-update) | async-done | bytes 24592
  377.6 0.8 copy.28
  378.5 61.4 %psum.7 = f32[3,32,128]{2,1,0:T(8,128)} all-reduce(bf16[3,32,128]{2,1,0:T(8,128)(2,1)S(1)} %bitcast.91), channel_id=1, replica_groups=mesh['dom'=16,'rep'=2] {'dom'}, use_global_device_ids=true, to_apply=%region_3.4 | all-reduce | flops 12288 | bytes 73728 | tf_op jit(solution)/shard_map/psum | solution.py:90
  (52 shorter events, 1.0 us)
Async XLA Ops:
  6.5 78.4 %copy-start = (f32[256,4,128]{2,1,0:T(4,128)S(1)}, f32[256,4,128]{2,1,0:T(4,128)}, u32[]{:S(2)}) copy-start(f32[256,4,128]{2,1,0:T(4,128)} %param.13) | copy-start | bytes 1572868
  6.5 371.1 %reduce-scatter.4.cloned.1.call-start = ((), (), s32[]{:S(2)}) async-start(), calls=%async_computation.1 | async-start | bytes 98304
  9.8 75.3 %copy-start.4 = (s32[256,128]{1,0:T(8,128)S(1)}, s32[256,128]{1,0:T(8,128)}, u32[]{:S(2)}) copy-start(s32[256,128]{1,0:T(8,128)} %param.12) | copy-start | bytes 393220
  9.8 75.4 %copy-start.2 = (s32[1792]{0:T(1024)S(1)}, s32[1792]{0:T(1024)}, u32[]{:S(2)}) copy-start(s32[1792]{0:T(1024)} %param.17) | copy-start | bytes 21508
  266.4 0.7 copy-start.1
  267.0 97.2 %copy-start.3 = (s32[256,128]{1,0:T(8,128)S(1)}, s32[256,128]{1,0:T(8,128)}, u32[]{:S(2)}) copy-start(s32[256,128]{1,0:T(8,128)} %param.11) | copy-start | bytes 393220
Sparse Core Ops, SparseCore 0:
  371.9 5.7 reduce-scatter.3
where the time goes:
time: 447 us
  local copies, waits for them, and re-layouts  282 us (63%)
  blocking collectives  136 us (30%)
  between operations  14.3 us (3%)
  waiting for transfers between devices  5.91 us (1%)
  matrix products  4.57 us (1%)
    gather x1, local copies, waits for them, and re-layouts, per_device(): jnp.take(store_region, store_key) * WEEKS + date_key // week_length  97.2 us
    gather x1, local copies, waits for them, and re-layouts, per_device(): day_ok = jnp.take(date_flag, date_key)  90.5 us
    gather x1, local copies, waits for them, and re-layouts, per_device(): price_row = jnp.take(prices, item_key)  90.5 us
    all_gather x1, blocking collectives, per_device(): prices = lax.all_gather(item_price, ('dom', 'rep'), axis=0, tiled=True)  75 us
    psum x1, blocking collectives, per_device(): totals = lax.psum(totals, 'dom')  61.4 us
  transfers between devices with their start and end apart: 1, of which 1 were waited for; matrix products, arithmetic and copies ran while one was open for 0% of the time, Pallas kernels for 0%

commit v1 on v0

v1 whole, which is shorter than its diff:
```python
import functools

import jax
import jax.numpy as jnp
import numpy as np
from jax import lax
from jax.experimental import pallas as pl
from jax.experimental.pallas import tpu as pltpu
from jax.sharding import PartitionSpec as P

MESH = pl.DeviceIdType.MESH
AGGS = 3
REG_DEV = 2
LANES = 128
low_price = 0.2
high_price = 0.8
week_length = 7


def round_up(value, step):
    return (value + step - 1) // step * step


def divider(divisor, limit):
    n = np.arange(limit, dtype=np.int64)
    for shift in range(8, 24):
        multiplier = -(-(1 << shift) // divisor)
        if (limit * multiplier) < (1 << 31) and np.array_equal((n * multiplier) >> shift, n // divisor):
            return multiplier, shift
    raise ValueError("no divider")


def lookup(row, lane):
    return jnp.take_along_axis(jnp.broadcast_to(row, lane.shape), lane, axis=1)


def kernel(
    dom_size, rep_size, regions, item_rows, slots, chunk,
    count_ref, date_hbm, item_hbm, store_hbm, meas_hbm, price_ref, region_ref, flag_ref,
    out_ref,
    date_v, item_v, store_v, meas_v, flags, words, reg_f, week_f, prof_f, rev_f, qty_f, lane_i, row_i, bit_i,
    acc, part, rbuf, fbuf,
    in_sem, z_send, z_recv, p_send, p_recv, q_send, q_recv, d_send, d_recv, c_send, c_recv,
    r_send, r_recv, f_send, f_recv,
):
    dom = lax.axis_index("dom")
    rep = lax.axis_index("rep")
    devices = dom_size * rep_size
    me = dom * rep_size + rep
    half = slots // rep_size
    outer_size = dom_size // 4
    outer = dom // 4
    mid = (dom // 2) % 2
    core = dom % 2

    base = pl.multiple_of(rep * half, 8)
    loads = [
        pltpu.make_async_copy(date_hbm.at[pl.ds(base, half)], date_v, in_sem.at[0]),
        pltpu.make_async_copy(item_hbm.at[pl.ds(base, half)], item_v, in_sem.at[1]),
        pltpu.make_async_copy(store_hbm.at[pl.ds(base, half)], store_v, in_sem.at[2]),
        pltpu.make_async_copy(meas_hbm.at[pl.ds(base * 4, half * 4)], meas_v, in_sem.at[3]),
    ]
    for load in loads:
        load.start()

    barrier = pltpu.get_barrier_semaphore()
    for k in range(1, devices):
        other = (me + k) % devices
        pl.semaphore_signal(
            barrier, inc=1, device_id={"dom": other // rep_size, "rep": other % rep_size}, device_id_type=MESH
        )

    padded = flags.shape[1]
    price = price_ref[...]
    power = jnp.left_shift(jnp.ones(price.shape, jnp.int32), me % 16).astype(jnp.float32)
    mark = jnp.where((price >= low_price) & (price <= high_price), power, 0.0)
    if padded > item_rows:
        mark = jnp.concatenate([mark, jnp.zeros((padded - item_rows, LANES), jnp.float32)], axis=0)
    flags[me] = mark.astype(jnp.bfloat16)
    pl.semaphore_wait(barrier, devices - 1)

    def index_of(o, m, c, r):
        return ((o * 2 + m) * 2 + c) * rep_size + r

    sends = []

    def send(block, to_dom, to_rep, s_sem, r_sem):
        copy = pltpu.make_async_remote_copy(
            src_ref=flags.at[block], dst_ref=flags.at[block], send_sem=s_sem, recv_sem=r_sem,
            device_id={"dom": to_dom, "rep": to_rep}, device_id_type=MESH,
        )
        copy.start()
        sends.append(copy)
        return copy

    dom_mid = dom + 2 - 4 * mid
    rep_other = (rep + 1) % rep_size
    dom_core = dom + 1 - 2 * core
    first_dom, first_rep = dom + (1 - core) * (2 - 4 * mid), rep + core * (rep_other - rep)
    second_dom, second_rep = dom + core * (2 - 4 * mid), rep + (1 - core) * (rep_other - rep)
    first_mid = mid + (1 - core) * (1 - 2 * mid)

    zc, pc, qc, dc, cc = {}, {}, {}, {}, {}

    def column(k):
        o = (outer + outer_size - k) % outer_size
        block = index_of(o, mid, core, rep)
        pc[k] = send(block, first_dom, first_rep, p_send.at[k], p_recv.at[k])
        qc[k] = send(block, second_dom, second_rep, q_send.at[k], q_recv.at[k])
        cc[0, k] = send(block, dom_core, rep, c_send.at[0, k], c_recv.at[0, k])

    def got_p(k):
        pc[k].wait_recv()
        o = (outer + outer_size - k) % outer_size
        block = index_of(o, first_mid, core, first_rep)
        dc[k] = send(block, second_dom, second_rep, d_send.at[k], d_recv.at[k])
        cc[1, k] = send(block, dom_core, rep, c_send.at[1, k], c_recv.at[1, k])

    def got_q(k):
        qc[k].wait_recv()
        o = (outer + outer_size - k) % outer_size
        second_mid = mid + core * (1 - 2 * mid)
        cc[2, k] = send(index_of(o, second_mid, core, second_rep), dom_core, rep, c_send.at[2, k], c_recv.at[2, k])

    def got_d(k):
        dc[k].wait_recv()
        o = (outer + outer_size - k) % outer_size
        cc[3, k] = send(index_of(o, 1 - mid, core, rep_other), dom_core, rep, c_send.at[3, k], c_recv.at[3, k])

    for k in range(1, outer_size):
        o = (outer + k) % outer_size
        zc[k] = send(me, o * 4 + dom % 4, rep, z_send.at[k - 1], z_recv.at[k - 1])
    column(0)

    for load in loads:
        load.wait()
    date_word = flag_ref[0:1, :]
    for j in range(1, flag_ref.shape[0]):
        date_word = date_word | (flag_ref[j : j + 1, :] << j)
    week_mul, week_shift = divider(week_length, flag_ref.shape[0] * LANES)
    dev_mul, dev_shift = divider(item_rows, item_rows * devices)
    count = count_ref[0]

    def prepare(g, carry):
        start = pl.multiple_of(g * 8, 8)
        rows = pl.ds(start, 8)
        date = date_v[rows, :]
        day = (lookup(date_word, date & (LANES - 1)) >> (date >> 7)) & 1
        store = store_v[rows, :]
        region = lookup(region_ref[0:1, :], store & (LANES - 1))
        for j in range(1, region_ref.shape[0]):
            region = jnp.where((store >> 7) == j, lookup(region_ref[j : j + 1, :], store & (LANES - 1)), region)
        slot = base + start + lax.broadcasted_iota(jnp.int32, (8, LANES), 0)
        ok = (day == 1) & (slot < count)
        reg_f[rows, :] = jnp.where(ok, region, -1).astype(jnp.float32)
        week_f[rows, :] = ((date * week_mul) >> week_shift).astype(jnp.float32)
        quantity = meas_v[pl.ds(start * 4, 8, stride=4), :]
        selling = meas_v[pl.ds(start * 4 + 1, 8, stride=4), :]
        wholesale = meas_v[pl.ds(start * 4 + 2, 8, stride=4), :]
        coupon = meas_v[pl.ds(start * 4 + 3, 8, stride=4), :]
        prof_f[rows, :] = quantity * (selling - wholesale) - coupon
        rev_f[rows, :] = quantity * selling - coupon
        qty_f[rows, :] = quantity
        item = item_v[rows, :]
        page = item >> 7
        holder = (page * dev_mul) >> dev_shift
        lane_i[rows, :] = item & (LANES - 1)
        row_i[rows, :] = (holder >> 5) * item_rows + page - holder * item_rows
        bit_i[rows, :] = holder & 31
        return carry

    lax.fori_loop(0, half // 8, prepare, 0)

    for k in range(outer_size):
        got_p(k)
        if k + 1 < outer_size:
            zc[k + 1].wait_recv()
            column(k + 1)
        got_q(k)
        if k >= 1:
            got_d(k - 1)
    got_d(outer_size - 1)
    for k in range(outer_size):
        for j in range(4):
            cc[j, k].wait_recv()

    for g in range((devices + 31) // 32):
        word = None
        for h in range(2):
            total = None
            for b in range(16):
                device = g * 32 + h * 16 + b
                if device < devices:
                    piece = flags[device].astype(jnp.float32)
                    total = piece if total is None else total + piece
            if total is not None:
                bits = total.astype(jnp.int32)
                word = bits if h == 0 else word | (bits << 16)
        words[g * item_rows : (g + 1) * item_rows, :] = word[:item_rows]

    acc[...] = jnp.zeros(acc.shape, jnp.float32)
    weeks = acc.shape[1]
    word_rows = words.shape[0]
    iota = lax.broadcasted_iota(jnp.int32, (16, LANES), 0).astype(jnp.float32)
    region_iota = [(iota + 16.0 * j).astype(jnp.bfloat16) for j in range(regions // 16)]
    week_iota = [(iota + 16.0 * j).astype(jnp.bfloat16) for j in range(weeks // 16)]
    zero = jnp.zeros((16, LANES), jnp.bfloat16)
    one = jnp.ones((16, LANES), jnp.bfloat16)

    def add_chunk(n, carry):
        first = pl.multiple_of(n * chunk, 8)
        for g in range(chunk // 8):
            rows = pl.ds(first + 8 * g, 8)
            lane, row = lane_i[rows, :], row_i[rows, :]
            found = lookup(words[0:1, :], lane)
            for w in range(1, word_rows):
                found = jnp.where(row == w, lookup(words[w : w + 1, :], lane), found)
            hit = (found >> bit_i[rows, :]) & 1
            reg_f[rows, :] = jnp.where(hit == 1, reg_f[rows, :], -1.0)
        lefts, rights = [], []
        for s in range(chunk):
            line = pl.ds(first + s, 1)

            def spread(ref):
                return jnp.broadcast_to(ref[line, :], (16, LANES)).astype(jnp.bfloat16)

            region, week = spread(reg_f), spread(week_f)
            values = [spread(prof_f), spread(rev_f), spread(qty_f)]
            masks = [one_iota == region for one_iota in region_iota]
            lefts.append(jnp.concatenate([jnp.where(m, v, zero) for v in values for m in masks], axis=0))
            rights.append(jnp.concatenate([jnp.where(w == week, one, zero) for w in week_iota], axis=0))
        left = jnp.concatenate(lefts, axis=1)
        right = jnp.concatenate(rights, axis=1)
        acc[...] += lax.dot_general(left, right, (((1,), (1,)), ((), ())), preferred_element_type=jnp.float32)
        return carry

    lax.fori_loop(0, half // chunk, add_chunk, 0)

    tile = fbuf.shape[1]
    tiles = fbuf.shape[0]
    cols = weeks // rep_size
    for j in range(rep_size):
        part[j] = acc[:, j * cols : (j + 1) * cols].astype(jnp.bfloat16)
    my_tile = (dom * tiles + dom_size - 1) // dom_size
    is_owner = jnp.logical_and(my_tile < tiles, (my_tile * dom_size) // tiles == dom)

    def partial_copy(t, j):
        owner = t * dom_size // tiles
        target = owner * rep_size + j
        slot = (me + devices - target) % devices
        return target, pltpu.make_async_remote_copy(
            src_ref=part.at[j, pl.ds(t * tile, tile)], dst_ref=rbuf.at[slot],
            send_sem=r_send.at[t, j], recv_sem=r_recv.at[slot],
            device_id={"dom": owner, "rep": j}, device_id_type=MESH,
        )

    for t in range(tiles):
        for j in range(rep_size):
            target, copy = partial_copy(t, j)

            @pl.when(target != me)
            def _():
                copy.start()

    def final_copy(k):
        other = (dom + k) % dom_size
        return pltpu.make_async_remote_copy(
            src_ref=fbuf.at[my_tile], dst_ref=fbuf.at[my_tile],
            send_sem=f_send.at[k], recv_sem=f_recv.at[my_tile],
            device_id={"dom": other, "rep": rep}, device_id_type=MESH,
        )

    @pl.when(is_owner)
    def _():
        total = part[rep, pl.ds(pl.multiple_of(my_tile * tile, tile), tile), :].astype(jnp.float32)
        for slot in range(1, devices):
            pltpu.make_async_copy(rbuf.at[slot], rbuf.at[slot], r_recv.at[slot]).wait()
            total = total + rbuf[slot].astype(jnp.float32)
        fbuf[my_tile] = total
        for k in range(1, dom_size):
            final_copy(k).start()

    for t in range(tiles):

        @pl.when(jnp.logical_not(jnp.logical_and(is_owner, my_tile == t)))
        def _():
            pltpu.make_async_copy(fbuf.at[t], fbuf.at[t], f_recv.at[t]).wait()

    out_ref[...] = fbuf[...]

    @pl.when(is_owner)
    def _():
        for k in range(1, dom_size):
            final_copy(k).wait_send()

    for t in range(tiles):
        for j in range(rep_size):
            target, copy = partial_copy(t, j)

            @pl.when(target != me)
            def _():
                copy.wait_send()

    for copy in sends:
        copy.wait_send()


def per_device(
    date_key, item_key, store_key, measures, block_count, item_price, store_region, date_flag
):
    dom_size = lax.axis_size("dom")
    rep_size = lax.axis_size("rep")
    devices = dom_size * rep_size
    regions = REG_DEV * dom_size
    weeks = date_flag.shape[0] // week_length
    slots = date_key.shape[0]
    half = slots // rep_size
    item_rows = item_price.shape[0] // LANES
    chunk = 16
    tile = 16
    tiles = AGGS * regions // tile
    outer = dom_size // 4
    bf16, f32, i32 = jnp.bfloat16, jnp.float32, jnp.int32
    dma = pltpu.SemaphoreType.DMA
    vmem = pl.BlockSpec(memory_space=pltpu.VMEM)
    hbm = pl.BlockSpec(memory_space=pl.ANY)
    facts = (half, LANES)
    out = pl.pallas_call(
        functools.partial(kernel, dom_size, rep_size, regions, item_rows, slots, chunk),
        out_shape=jax.ShapeDtypeStruct((tiles, tile, weeks // rep_size), f32),
        in_specs=[pl.BlockSpec(memory_space=pltpu.SMEM), hbm, hbm, hbm, hbm, vmem, vmem, vmem],
        out_specs=vmem,
        scratch_shapes=[
            pltpu.VMEM(facts, i32), pltpu.VMEM(facts, i32), pltpu.VMEM(facts, i32),
            pltpu.VMEM((half * 4, LANES), f32),
            pltpu.VMEM((devices, round_up(item_rows, 16), LANES), bf16),
            pltpu.VMEM(((devices + 31) // 32 * item_rows, LANES), i32),
            pltpu.VMEM(facts, f32), pltpu.VMEM(facts, f32), pltpu.VMEM(facts, f32),
            pltpu.VMEM(facts, f32), pltpu.VMEM(facts, f32),
            pltpu.VMEM(facts, i32), pltpu.VMEM(facts, i32), pltpu.VMEM(facts, i32),
            pltpu.VMEM((AGGS * regions, weeks), f32),
            pltpu.VMEM((rep_size, AGGS * regions, weeks // rep_size), bf16),
            pltpu.VMEM((devices, tile, weeks // rep_size), bf16),
            pltpu.VMEM((tiles, tile, weeks // rep_size), f32),
            dma((4,)),
            dma((outer - 1,)), dma((outer - 1,)),
            dma((outer,)), dma((outer,)), dma((outer,)), dma((outer,)), dma((outer,)), dma((outer,)),
            dma((4, outer)), dma((4, outer)),
            dma((tiles, rep_size)), dma((devices,)),
            dma((dom_size,)), dma((tiles,)),
        ],
        compiler_params=pltpu.CompilerParams(
            collective_id=0, has_side_effects=True, vmem_limit_bytes=40 * 1024 * 1024
        ),
        cost_estimate=pl.CostEstimate(
            flops=2 * AGGS * regions * weeks * half * LANES, bytes_accessed=half * LANES * 28, transcendentals=0
        ),
    )(
        block_count, date_key, item_key, store_key, measures.reshape(slots * 4, LANES),
        item_price.reshape(item_rows, LANES), store_region.reshape(-1, LANES), date_flag.reshape(-1, LANES),
    )
    return out.reshape(AGGS, regions, weeks // rep_size)


def solution(mesh):
    placed = (
        P("dom", None),
        P("dom", None),
        P("dom", None),
        P("dom", None, None),
        P("dom"),
        P(("dom", "rep")),
        P(),
        P(),
    )
    return jax.shard_map(
        per_device, mesh=mesh, in_specs=placed, out_specs=P(None, None, "rep"), check_vma=False
    )
```

time: 447 us -> 42 us (0.09)
  local copies, waits for them, and re-layouts: 282 us -> 5.77 us
  blocking collectives: 136 us -> 0 us
  Pallas kernels: 0 us -> 35.2 us
  between operations: 14.3 us -> 0.69 us
  waiting for transfers between devices: 5.91 us -> 0 us
  matrix products: 4.57 us -> 0 us
    gather x3 -> x0, local copies, waits for them, and re-layouts: 278 us -> none  [the longest x1 97.2 us: per_device(): jnp.take(store_region, store_key) * WEEKS + date_key // week_length]
    all_gather x1 -> x0, blocking collectives: 75 us -> none  [per_device(): prices = lax.all_gather(item_price, ('dom', 'rep'), axis=0, tiled=True)]
    psum x1 -> x0, blocking collectives: 61.4 us -> none  [per_device(): totals = lax.psum(totals, 'dom')]
    pallas_call x0 -> x1, Pallas kernels: none -> 35.2 us  [per_device(): pl.pallas_call(functools.partial(kernel, dom_size, rep_size, regions, ite...]
    unnamed x2 -> x0, waiting for transfers between devices: 5.91 us -> none
    dot_general x8 -> x0, matrix products: 4.57 us -> none  [add_step(): jnp.dot(left_side, week_hot, preferred_element_type=jnp.float32)]
  transfers between devices with their start and end apart: 1 -> 0, of which waited for: 1 -> 0; matrix products, arithmetic and copies ran while one was open for 0% -> 0% of each run, Pallas kernels for 0% -> 0%
where the time goes in v1:
time: 42 us; the launch traced here: 41.7 us
  Pallas kernels  35.2 us (84%)
  local copies, waits for them, and re-layouts  5.77 us (14%)
  between operations  0.69 us (2%)
    pallas_call x1, Pallas kernels, per_device(): pl.pallas_call(functools.partial(kernel, dom_size, rep_size, regions, ite...  35.2 us
    unnamed x15, local copies, waits for them, and re-layouts  5.77 us

profile of v1, /device:TPU:0, one launch (start us, length us, event | category | flops | bytes accessed | tf_op | source)
XLA Modules:
  0.0 41.7 jit_solution(13103043953366743266)
XLA Ops:
  0.0 0.0 copy-start.5
  0.7 0.0 copy-start.6
  0.7 0.0 copy-done.5
  0.7 0.6 %copy-done.6 = s32[128]{0:T(128)S(1)} copy-done((s32[128]{0:T(128)S(1)}, s32[128]{0:T(128)}, u32[]{:S(2)}) %copy-start.6) | copy-done | bytes 536
  1.3 0.0 copy-start
  1.3 1.0 %copy-done = f32[256,4,128]{2,1,0:T(4,128)S(1)} copy-done((f32[256,4,128]{2,1,0:T(4,128)S(1)}, f32[256,4,128]{2,1,0:T(4,128)}, u32[]{:S(2)}) %copy-start) | copy-done | bytes 524312
  2.4 0.0 copy-start.1
  2.4 0.9 %copy-done.1 = s32[256,128]{1,0:T(8,128)S(1)} copy-done((s32[256,128]{1,0:T(8,128)S(1)}, s32[256,128]{1,0:T(8,128)}, u32[]{:S(2)}) %copy-start.1) | copy-done | bytes 131096
  3.3 0.0 copy-start.2
  3.3 0.9 %copy-done.2 = s32[256,128]{1,0:T(8,128)S(1)} copy-done((s32[256,128]{1,0:T(8,128)S(1)}, s32[256,128]{1,0:T(8,128)}, u32[]{:S(2)}) %copy-start.2) | copy-done | bytes 131096
  4.2 0.0 copy-start.3
  4.2 0.9 %copy-done.3 = s32[256,128]{1,0:T(8,128)S(1)} copy-done((s32[256,128]{1,0:T(8,128)S(1)}, s32[256,128]{1,0:T(8,128)}, u32[]{:S(2)}) %copy-start.3) | copy-done | bytes 131096
  5.1 0.0 copy-start.4
  5.1 0.7 %copy-done.4 = f32[7168]{0:T(1024)S(1)} copy-done((f32[7168]{0:T(1024)S(1)}, f32[7168]{0:T(1024)}, u32[]{:S(2)}) %copy-start.4) | copy-done | bytes 28696
  5.8 35.2 %shard_map.82 = f32[6,16,128]{2,1,0:T(8,128)S(1)} custom-call(s32[1]{0:T(128)S(6)} %copy.10.count_ref, s32[256,128]{1,0:T(8,128)S(1)} %copy-done.1, s32[256,128]{1,0:T(8,128)S(1)} %copy-done.2, s32[256,128]{1,0:T(8,128)S(1)} %copy-done.3, f32[1024,128]{1,0:T(8,128)S(1)} %bitcast.6, f32[56,128]{1,0:T(8,128)S(1)} %bitcast.7, s32[1,128]{1,0:T(1,128)S(1)} %bitcast.9, ...), custom_call_target="tpu_custom_call" | custom-call | flops 805306368 | bytes 458752 | tf_op jit(solution)/shard_map/pallas_call | solution.py:328
  41.1 0.6 %copy.11 = f32[3,32,128]{2,1,0:T(8,128)} copy(f32[3,32,128]{2,1,0:T(8,128)S(1)} %bitcast.5) | data formatting | bytes 98304
Async XLA Ops:
  0.0 0.7 %copy-start.5 = (s32[1792]{0:T(1024)S(1)}, s32[1792]{0:T(1024)}, u32[]{:S(2)}) copy-start(s32[1792]{0:T(1024)} %param.15) | copy-start | bytes 21508
  0.7 0.7 %copy-start.6 = (s32[128]{0:T(128)S(1)}, s32[128]{0:T(128)}, u32[]{:S(2)}) copy-start(s32[128]{0:T(128)} %param.14) | copy-start | bytes 1540
  1.3 1.0 %copy-start = (f32[256,4,128]{2,1,0:T(4,128)S(1)}, f32[256,4,128]{2,1,0:T(4,128)}, u32[]{:S(2)}) copy-start(f32[256,4,128]{2,1,0:T(4,128)} %param.11) | copy-start | bytes 1572868
  2.4 0.9 %copy-start.1 = (s32[256,128]{1,0:T(8,128)S(1)}, s32[256,128]{1,0:T(8,128)}, u32[]{:S(2)}) copy-start(s32[256,128]{1,0:T(8,128)} %date_hbm.1) | copy-start | bytes 393220
  3.3 0.9 %copy-start.2 = (s32[256,128]{1,0:T(8,128)S(1)}, s32[256,128]{1,0:T(8,128)}, u32[]{:S(2)}) copy-start(s32[256,128]{1,0:T(8,128)} %item_hbm.1) | copy-start | bytes 393220
  4.2 0.9 %copy-start.3 = (s32[256,128]{1,0:T(8,128)S(1)}, s32[256,128]{1,0:T(8,128)}, u32[]{:S(2)}) copy-start(s32[256,128]{1,0:T(8,128)} %store_hbm.1) | copy-start | bytes 393220
  5.1 0.7 %copy-start.4 = (f32[7168]{0:T(1024)S(1)}, f32[7168]{0:T(1024)}, u32[]{:S(2)}) copy-start(f32[7168]{0:T(1024)} %param.13) | copy-start | bytes 86020

commit v2 on v1

--- a/solution.py
+++ b/solution.py
@@ -36,9 +36,10 @@
 
 def kernel(
     dom_size, rep_size, regions, item_rows, slots, chunk,
-    count_ref, date_hbm, item_hbm, store_hbm, meas_hbm, price_ref, region_ref, flag_ref,
+    count_ref, date_hbm, item_hbm, store_hbm, meas_hbm, price_hbm, region_hbm, flag_hbm,
     out_ref,
-    date_v, item_v, store_v, meas_v, flags, words, reg_f, week_f, prof_f, rev_f, qty_f, lane_i, row_i, bit_i,
+    date_v, item_v, store_v, meas_v, price_ref, region_ref, flag_ref,
+    flags, words, reg_f, hit_f, week_f, prof_f, rev_f, qty_f, lane_i, row_i, bit_i, week_hot,
     acc, part, rbuf, fbuf,
     in_sem, z_send, z_recv, p_send, p_recv, q_send, q_recv, d_send, d_recv, c_send, c_recv,
     r_send, r_recv, f_send, f_recv,
@@ -54,11 +55,15 @@
     core = dom % 2
 
     base = pl.multiple_of(rep * half, 8)
+    price_load = pltpu.make_async_copy(price_hbm, price_ref, in_sem.at[4])
+    price_load.start()
     loads = [
         pltpu.make_async_copy(date_hbm.at[pl.ds(base, half)], date_v, in_sem.at[0]),
         pltpu.make_async_copy(item_hbm.at[pl.ds(base, half)], item_v, in_sem.at[1]),
         pltpu.make_async_copy(store_hbm.at[pl.ds(base, half)], store_v, in_sem.at[2]),
         pltpu.make_async_copy(meas_hbm.at[pl.ds(base * 4, half * 4)], meas_v, in_sem.at[3]),
+        pltpu.make_async_copy(region_hbm, region_ref, in_sem.at[5]),
+        pltpu.make_async_copy(flag_hbm, flag_ref, in_sem.at[6]),
     ]
     for load in loads:
         load.start()
@@ -71,6 +76,7 @@
         )
 
     padded = flags.shape[1]
+    price_load.wait()
     price = price_ref[...]
     power = jnp.left_shift(jnp.ones(price.shape, jnp.int32), me % 16).astype(jnp.float32)
     mark = jnp.where((price >= low_price) & (price <= high_price), power, 0.0)
@@ -140,6 +146,8 @@
     week_mul, week_shift = divider(week_length, flag_ref.shape[0] * LANES)
     dev_mul, dev_shift = divider(item_rows, item_rows * devices)
     count = count_ref[0]
+    cols = week_hot.shape[1]
+    mid_group = regions * rep_size // 2
 
     def prepare(g, carry):
         start = pl.multiple_of(g * 8, 8)
@@ -152,8 +160,12 @@
             region = jnp.where((store >> 7) == j, lookup(region_ref[j : j + 1, :], store & (LANES - 1)), region)
         slot = base + start + lax.broadcasted_iota(jnp.int32, (8, LANES), 0)
         ok = (day == 1) & (slot < count)
-        reg_f[rows, :] = jnp.where(ok, region, -1).astype(jnp.float32)
-        week_f[rows, :] = ((date * week_mul) >> week_shift).astype(jnp.float32)
+        week = (date * week_mul) >> week_shift
+        part_of = jnp.zeros(week.shape, jnp.int32)
+        for j in range(1, rep_size):
+            part_of = jnp.where(week >= j * cols, j, part_of)
+        reg_f[rows, :] = jnp.where(ok, part_of * regions + region - mid_group, mid_group).astype(jnp.float32)
+        week_f[rows, :] = (week - part_of * cols).astype(jnp.float32)
         quantity = meas_v[pl.ds(start * 4, 8, stride=4), :]
         selling = meas_v[pl.ds(start * 4 + 1, 8, stride=4), :]
         wholesale = meas_v[pl.ds(start * 4 + 2, 8, stride=4), :]
@@ -171,15 +183,35 @@
 
     lax.fori_loop(0, half // 8, prepare, 0)
 
+    column_iota = lax.broadcasted_iota(jnp.int32, (LANES, cols), 1).astype(jnp.float32)
+
+    def build_weeks(n):
+        turned = jnp.transpose(week_f[n * chunk : (n + 1) * chunk, :])
+        for i in range(chunk):
+            hot = jnp.where(turned[:, i : i + 1] == column_iota, 1.0, 0.0).astype(jnp.bfloat16)
+            week_hot[(n * chunk + i) * LANES : (n * chunk + i + 1) * LANES, :] = hot
+
+    chunks = half // chunk
+    to_build = list(range(chunks))
+
+    def idle():
+        if to_build:
+            build_weeks(to_build.pop(0))
+
     for k in range(outer_size):
         got_p(k)
+        idle()
         if k + 1 < outer_size:
             zc[k + 1].wait_recv()
             column(k + 1)
+            idle()
         got_q(k)
+        idle()
         if k >= 1:
             got_d(k - 1)
     got_d(outer_size - 1)
+    while to_build:
+        idle()
     for k in range(outer_size):
         for j in range(4):
             cc[j, k].wait_recv()
@@ -199,16 +231,16 @@
         words[g * item_rows : (g + 1) * item_rows, :] = word[:item_rows]
 
     acc[...] = jnp.zeros(acc.shape, jnp.float32)
-    weeks = acc.shape[1]
     word_rows = words.shape[0]
+    groups = regions * rep_size
     iota = lax.broadcasted_iota(jnp.int32, (16, LANES), 0).astype(jnp.float32)
-    region_iota = [(iota + 16.0 * j).astype(jnp.bfloat16) for j in range(regions // 16)]
-    week_iota = [(iota + 16.0 * j).astype(jnp.bfloat16) for j in range(weeks // 16)]
+    group_iota = [(iota + (16.0 * j - mid_group)).astype(jnp.bfloat16) for j in range(groups // 16)]
+    per_part = regions // 16
     zero = jnp.zeros((16, LANES), jnp.bfloat16)
-    one = jnp.ones((16, LANES), jnp.bfloat16)
-
-    def add_chunk(n, carry):
+
+    def hits(n):
         first = pl.multiple_of(n * chunk, 8)
+        found_all = []
         for g in range(chunk // 8):
             rows = pl.ds(first + 8 * g, 8)
             lane, row = lane_i[rows, :], row_i[rows, :]
@@ -216,31 +248,52 @@
             for w in range(1, word_rows):
                 found = jnp.where(row == w, lookup(words[w : w + 1, :], lane), found)
             hit = (found >> bit_i[rows, :]) & 1
-            reg_f[rows, :] = jnp.where(hit == 1, reg_f[rows, :], -1.0)
-        lefts, rights = [], []
-        for s in range(chunk):
-            line = pl.ds(first + s, 1)
-
-            def spread(ref):
-                return jnp.broadcast_to(ref[line, :], (16, LANES)).astype(jnp.bfloat16)
-
-            region, week = spread(reg_f), spread(week_f)
-            values = [spread(prof_f), spread(rev_f), spread(qty_f)]
-            masks = [one_iota == region for one_iota in region_iota]
-            lefts.append(jnp.concatenate([jnp.where(m, v, zero) for v in values for m in masks], axis=0))
-            rights.append(jnp.concatenate([jnp.where(w == week, one, zero) for w in week_iota], axis=0))
+            found_all.append(jnp.where(hit == 1, reg_f[rows, :], float(mid_group)))
+        return found_all
+
+    def put(slot, found_all):
+        for g in range(chunk // 8):
+            hit_f[slot, 8 * g : 8 * g + 8, :] = found_all[g]
+
+    put(0, hits(0))
+
+    def add_chunk(n, carry):
+        first = pl.multiple_of(n * chunk, 8)
+        ahead = hits(jnp.minimum(n + 1, chunks - 1))
+        lefts = []
+        for i in range(chunk):
+
+            def spread(row):
+                return jnp.broadcast_to(row, (16, LANES)).astype(jnp.bfloat16)
+
+            group = spread(hit_f[n % 2, i : i + 1, :])
+            line = pl.ds(first + i, 1)
+            values = [spread(prof_f[line, :]), spread(rev_f[line, :]), spread(qty_f[line, :])]
+            masks = [one_iota == group for one_iota in group_iota]
+            lefts.append(
+                jnp.concatenate(
+                    [
+                        jnp.where(m, v, zero)
+                        for j in range(rep_size)
+                        for v in values
+                        for m in masks[j * per_part : (j + 1) * per_part]
+                    ],
+                    axis=0,
+                )
+            )
         left = jnp.concatenate(lefts, axis=1)
-        right = jnp.concatenate(rights, axis=1)
-        acc[...] += lax.dot_general(left, right, (((1,), (1,)), ((), ())), preferred_element_type=jnp.float32)
+        right = week_hot[pl.ds(pl.multiple_of(first * LANES, LANES), chunk * LANES), :]
+        acc[...] += jnp.dot(left, right, preferred_element_type=jnp.float32)
+        put((n + 1) % 2, ahead)
         return carry
 
-    lax.fori_loop(0, half // chunk, add_chunk, 0)
+    lax.fori_loop(0, chunks, add_chunk, 0)
 
     tile = fbuf.shape[1]
     tiles = fbuf.shape[0]
-    cols = weeks // rep_size
+    out_rows = AGGS * regions
     for j in range(rep_size):
-        part[j] = acc[:, j * cols : (j + 1) * cols].astype(jnp.bfloat16)
+        part[j] = acc[j * out_rows : (j + 1) * out_rows, :].astype(jnp.bfloat16)
     my_tile = (dom * tiles + dom_size - 1) // dom_size
     is_owner = jnp.logical_and(my_tile < tiles, (my_tile * dom_size) // tiles == dom)
 
@@ -328,21 +381,25 @@
     out = pl.pallas_call(
         functools.partial(kernel, dom_size, rep_size, regions, item_rows, slots, chunk),
         out_shape=jax.ShapeDtypeStruct((tiles, tile, weeks // rep_size), f32),
-        in_specs=[pl.BlockSpec(memory_space=pltpu.SMEM), hbm, hbm, hbm, hbm, vmem, vmem, vmem],
+        in_specs=[pl.BlockSpec(memory_space=pltpu.SMEM), hbm, hbm, hbm, hbm, hbm, hbm, hbm],
         out_specs=vmem,
         scratch_shapes=[
             pltpu.VMEM(facts, i32), pltpu.VMEM(facts, i32), pltpu.VMEM(facts, i32),
             pltpu.VMEM((half * 4, LANES), f32),
+            pltpu.VMEM((item_rows, LANES), f32),
+            pltpu.VMEM((store_region.shape[0] // LANES, LANES), i32),
+            pltpu.VMEM((date_flag.shape[0] // LANES, LANES), i32),
             pltpu.VMEM((devices, round_up(item_rows, 16), LANES), bf16),
             pltpu.VMEM(((devices + 31) // 32 * item_rows, LANES), i32),
-            pltpu.VMEM(facts, f32), pltpu.VMEM(facts, f32), pltpu.VMEM(facts, f32),
-            pltpu.VMEM(facts, f32), pltpu.VMEM(facts, f32),
+            pltpu.VMEM(facts, f32), pltpu.VMEM((2, chunk, LANES), f32),
+            pltpu.VMEM(facts, f32), pltpu.VMEM(facts, f32), pltpu.VMEM(facts, f32), pltpu.VMEM(facts, f32),
             pltpu.VMEM(facts, i32), pltpu.VMEM(facts, i32), pltpu.VMEM(facts, i32),
-            pltpu.VMEM((AGGS * regions, weeks), f32),
+            pltpu.VMEM((half * LANES, weeks // rep_size), bf16),
+            pltpu.VMEM((rep_size * AGGS * regions, weeks // rep_size), f32),
             pltpu.VMEM((rep_size, AGGS * regions, weeks // rep_size), bf16),
             pltpu.VMEM((devices, tile, weeks // rep_size), bf16),
             pltpu.VMEM((tiles, tile, weeks // rep_size), f32),
-            dma((4,)),
+            dma((7,)),
             dma((outer - 1,)), dma((outer - 1,)),
             dma((outer,)), dma((outer,)), dma((outer,)), dma((outer,)), dma((outer,)), dma((outer,)),
             dma((4, outer)), dma((4, outer)),
@@ -350,7 +407,7 @@
             dma((dom_size,)), dma((tiles,)),
         ],
         compiler_params=pltpu.CompilerParams(
-            collective_id=0, has_side_effects=True, vmem_limit_bytes=40 * 1024 * 1024
+            collective_id=0, has_side_effects=True, vmem_limit_bytes=60 * 1024 * 1024
         ),
         cost_estimate=pl.CostEstimate(
             flops=2 * AGGS * regions * weeks * half * LANES, bytes_accessed=half * LANES * 28, transcendentals=0

time: 42 us -> 37.7 us (0.90)
  local copies, waits for them, and re-layouts: 5.77 us -> 1.42 us
    unnamed x15 -> x1, local copies, waits for them, and re-layouts: 5.77 us -> 1.42 us
where the time goes in v2:
time: 37.7 us; the launch traced here: 37.5 us
  Pallas kernels  35.4 us (94%)
  local copies, waits for them, and re-layouts  1.42 us (4%)
  between operations  0.66 us (2%)
    pallas_call x1, Pallas kernels, per_device(): pl.pallas_call(functools.partial(kernel, dom_size, rep_size, regions, ite...  35.4 us
    unnamed x1, local copies, waits for them, and re-layouts  1.42 us

profile of v2, /device:TPU:0, one launch (start us, length us, event | category | flops | bytes accessed | tf_op | source)
XLA Modules:
  0.0 37.5 jit_solution(6828514874242977760)
XLA Ops:
  0.7 35.4 %shard_map.82 = f32[6,16,128]{2,1,0:T(8,128)} custom-call(s32[1]{0:T(128)S(6)} %copy.10.count_ref, s32[256,128]{1,0:T(8,128)} %date_hbm.1, s32[256,128]{1,0:T(8,128)} %item_hbm.1, s32[256,128]{1,0:T(8,128)} %store_hbm.1, f32[1024,128]{1,0:T(8,128)} %bitcast.6, f32[56,128]{1,0:T(8,128)} %bitcast.7, s32[1,128]{1,0:T(1,128)} %bitcast.9, s32[14,128]{1,0:T(8,128)} %bitcast.8), custom_call_target="tpu_custom_call" | custom-call | flops 805306368 | bytes 458752 | tf_op jit(solution)/shard_map/pallas_call | solution.py:381
  36.1 1.4 %copy.11 = f32[3,32,128]{2,1,0:T(8,128)} copy(f32[3,32,128]{2,1,0:T(8,128)} %bitcast.5) | data formatting | bytes 98304

commit v3 on v2

--- a/solution.py
+++ b/solution.py
@@ -39,7 +39,7 @@
     count_ref, date_hbm, item_hbm, store_hbm, meas_hbm, price_hbm, region_hbm, flag_hbm,
     out_ref,
     date_v, item_v, store_v, meas_v, price_ref, region_ref, flag_ref,
-    flags, words, reg_f, hit_f, week_f, prof_f, rev_f, qty_f, lane_i, row_i, bit_i, week_hot,
+    flags, words, reg_f, week_f, prof_f, rev_f, qty_f, lane_i, row_i, bit_i, found_i, left_hot,
     acc, part, rbuf, fbuf,
     in_sem, z_send, z_recv, p_send, p_recv, q_send, q_recv, d_send, d_recv, c_send, c_recv,
     r_send, r_recv, f_send, f_recv,
@@ -78,7 +78,11 @@
     padded = flags.shape[1]
     price_load.wait()
     price = price_ref[...]
-    power = jnp.left_shift(jnp.ones(price.shape, jnp.int32), me % 16).astype(jnp.float32)
+    shards = 4 * rep_size
+    bands = padded // 16
+    row_of = lax.broadcasted_iota(jnp.int32, price.shape, 0)
+    place = ((me % shards) * bands + (row_of >> 4)) & 15
+    power = jnp.left_shift(jnp.ones(price.shape, jnp.int32), place).astype(jnp.float32)
     mark = jnp.where((price >= low_price) & (price <= high_price), power, 0.0)
     if padded > item_rows:
         mark = jnp.concatenate([mark, jnp.zeros((padded - item_rows, LANES), jnp.float32)], axis=0)
@@ -144,9 +148,10 @@
     for j in range(1, flag_ref.shape[0]):
         date_word = date_word | (flag_ref[j : j + 1, :] << j)
     week_mul, week_shift = divider(week_length, flag_ref.shape[0] * LANES)
+    shard_mul, shard_shift = divider(shards, devices)
     dev_mul, dev_shift = divider(item_rows, item_rows * devices)
     count = count_ref[0]
-    cols = week_hot.shape[1]
+    cols = acc.shape[1]
     mid_group = regions * rep_size // 2
 
     def prepare(g, carry):
@@ -177,26 +182,81 @@
         page = item >> 7
         holder = (page * dev_mul) >> dev_shift
         lane_i[rows, :] = item & (LANES - 1)
-        row_i[rows, :] = (holder >> 5) * item_rows + page - holder * item_rows
-        bit_i[rows, :] = holder & 31
+        row = page - holder * item_rows
+        far = (holder * shard_mul) >> shard_shift
+        row_i[rows, :] = far * 16 + (row & 15)
+        bit_i[rows, :] = (holder - far * shards) * bands + (row >> 4)
+        found_i[rows, :] = jnp.zeros((8, LANES), jnp.int32)
         return carry
 
     lax.fori_loop(0, half // 8, prepare, 0)
 
-    column_iota = lax.broadcasted_iota(jnp.int32, (LANES, cols), 1).astype(jnp.float32)
-
-    def build_weeks(n):
-        turned = jnp.transpose(week_f[n * chunk : (n + 1) * chunk, :])
+    groups = regions * rep_size
+    iota = lax.broadcasted_iota(jnp.int32, (16, LANES), 0).astype(jnp.float32)
+    group_iota = [(iota + (16.0 * j - mid_group)).astype(jnp.bfloat16) for j in range(groups // 16)]
+    week_iota = [(iota + 16.0 * j).astype(jnp.bfloat16) for j in range(cols // 16)]
+    per_part = regions // 16
+    zero = jnp.zeros((16, LANES), jnp.bfloat16)
+    one = jnp.ones((16, LANES), jnp.bfloat16)
+    chunks = half // chunk
+    prebuilt = left_hot.shape[0] == chunks
+
+    def spread(ref, line):
+        return jnp.broadcast_to(ref[line, :], (16, LANES)).astype(jnp.bfloat16)
+
+    def left_tiles(line):
+        group = spread(reg_f, line)
+        values = [spread(prof_f, line), spread(rev_f, line), spread(qty_f, line)]
+        masks = [one_iota == group for one_iota in group_iota]
+        return [
+            jnp.where(m, v, zero)
+            for j in range(rep_size)
+            for v in values
+            for m in masks[j * per_part : (j + 1) * per_part]
+        ]
+
+    def build_left(n, at):
         for i in range(chunk):
-            hot = jnp.where(turned[:, i : i + 1] == column_iota, 1.0, 0.0).astype(jnp.bfloat16)
-            week_hot[(n * chunk + i) * LANES : (n * chunk + i + 1) * LANES, :] = hot
-
-    chunks = half // chunk
-    to_build = list(range(chunks))
-
-    def idle():
-        if to_build:
-            build_weeks(to_build.pop(0))
+            tiles_of = left_tiles(pl.ds(n * chunk + i, 1))
+            for j, values in enumerate(tiles_of):
+                left_hot[at, 16 * j : 16 * j + 16, i * LANES : (i + 1) * LANES] = values
+
+    to_build = list(range(chunks)) if prebuilt else []
+
+    def idle(amount=1):
+        for _ in range(amount):
+            if to_build:
+                n = to_build.pop(0)
+                build_left(n, n)
+
+    word_rows = min(16, item_rows)
+
+    def look_up(k):
+        for j in range(4):
+            cc[j, k].wait_recv()
+        o = (outer + outer_size - k) % outer_size
+        halves = [None, None]
+        for s in range(shards):
+            for q in range(bands):
+                piece = flags[o * shards + s, 16 * q : 16 * q + 16, :].astype(jnp.float32)
+                h = (s * bands + q) // 16
+                halves[h] = piece if halves[h] is None else halves[h] + piece
+        word = halves[0].astype(jnp.int32)
+        if halves[1] is not None:
+            word = word | (halves[1].astype(jnp.int32) << 16)
+        words[k % 2] = word
+
+        def look(g, carry):
+            for u in range(2):
+                rows = pl.ds(pl.multiple_of(g * 16 + 8 * u, 8), 8)
+                lane, row = lane_i[rows, :], row_i[rows, :] - o * 16
+                found = found_i[rows, :]
+                for w in range(word_rows):
+                    found = jnp.where(row == w, lookup(words[k % 2, w : w + 1, :], lane), found)
+                found_i[rows, :] = found
+            return carry
+
+        lax.fori_loop(0, half // 16, look, 0)
 
     for k in range(outer_size):
         got_p(k)
@@ -207,84 +267,29 @@
             idle()
         got_q(k)
         idle()
+        got_d(k)
         if k >= 1:
-            got_d(k - 1)
-    got_d(outer_size - 1)
-    while to_build:
-        idle()
-    for k in range(outer_size):
-        for j in range(4):
-            cc[j, k].wait_recv()
-
-    for g in range((devices + 31) // 32):
-        word = None
-        for h in range(2):
-            total = None
-            for b in range(16):
-                device = g * 32 + h * 16 + b
-                if device < devices:
-                    piece = flags[device].astype(jnp.float32)
-                    total = piece if total is None else total + piece
-            if total is not None:
-                bits = total.astype(jnp.int32)
-                word = bits if h == 0 else word | (bits << 16)
-        words[g * item_rows : (g + 1) * item_rows, :] = word[:item_rows]
+            look_up(k - 1)
+    idle(chunks)
+    look_up(outer_size - 1)
 
     acc[...] = jnp.zeros(acc.shape, jnp.float32)
-    word_rows = words.shape[0]
-    groups = regions * rep_size
-    iota = lax.broadcasted_iota(jnp.int32, (16, LANES), 0).astype(jnp.float32)
-    group_iota = [(iota + (16.0 * j - mid_group)).astype(jnp.bfloat16) for j in range(groups // 16)]
-    per_part = regions // 16
-    zero = jnp.zeros((16, LANES), jnp.bfloat16)
-
-    def hits(n):
+
+    def add_chunk(n, carry):
         first = pl.multiple_of(n * chunk, 8)
-        found_all = []
         for g in range(chunk // 8):
             rows = pl.ds(first + 8 * g, 8)
-            lane, row = lane_i[rows, :], row_i[rows, :]
-            found = lookup(words[0:1, :], lane)
-            for w in range(1, word_rows):
-                found = jnp.where(row == w, lookup(words[w : w + 1, :], lane), found)
-            hit = (found >> bit_i[rows, :]) & 1
-            found_all.append(jnp.where(hit == 1, reg_f[rows, :], float(mid_group)))
-        return found_all
-
-    def put(slot, found_all):
-        for g in range(chunk // 8):
-            hit_f[slot, 8 * g : 8 * g + 8, :] = found_all[g]
-
-    put(0, hits(0))
-
-    def add_chunk(n, carry):
-        first = pl.multiple_of(n * chunk, 8)
-        ahead = hits(jnp.minimum(n + 1, chunks - 1))
-        lefts = []
+            hit = (found_i[rows, :] >> bit_i[rows, :]) & 1
+            week_f[rows, :] = jnp.where(hit == 1, week_f[rows, :], -1.0)
+        rights = []
         for i in range(chunk):
-
-            def spread(row):
-                return jnp.broadcast_to(row, (16, LANES)).astype(jnp.bfloat16)
-
-            group = spread(hit_f[n % 2, i : i + 1, :])
-            line = pl.ds(first + i, 1)
-            values = [spread(prof_f[line, :]), spread(rev_f[line, :]), spread(qty_f[line, :])]
-            masks = [one_iota == group for one_iota in group_iota]
-            lefts.append(
-                jnp.concatenate(
-                    [
-                        jnp.where(m, v, zero)
-                        for j in range(rep_size)
-                        for v in values
-                        for m in masks[j * per_part : (j + 1) * per_part]
-                    ],
-                    axis=0,
-                )
-            )
-        left = jnp.concatenate(lefts, axis=1)
-        right = week_hot[pl.ds(pl.multiple_of(first * LANES, LANES), chunk * LANES), :]
-        acc[...] += jnp.dot(left, right, preferred_element_type=jnp.float32)
-        put((n + 1) % 2, ahead)
+            week = spread(week_f, pl.ds(first + i, 1))
+            rights.append(jnp.concatenate([jnp.where(w == week, one, zero) for w in week_iota], axis=0))
+        right = jnp.concatenate(rights, axis=1)
+        if not prebuilt:
+            build_left(n, 0)
+        left = left_hot[n if prebuilt else 0]
+        acc[...] += lax.dot_general(left, right, (((1,), (1,)), ((), ())), preferred_element_type=jnp.float32)
         return carry
 
     lax.fori_loop(0, chunks, add_chunk, 0)
@@ -373,6 +378,8 @@
     tile = 16
     tiles = AGGS * regions // tile
     outer = dom_size // 4
+    left_bytes = rep_size * AGGS * regions * half * LANES * 2
+    prebuilt = half // chunk if left_bytes <= 24 * 1024 * 1024 else 1
     bf16, f32, i32 = jnp.bfloat16, jnp.float32, jnp.int32
     dma = pltpu.SemaphoreType.DMA
     vmem = pl.BlockSpec(memory_space=pltpu.VMEM)
@@ -390,11 +397,12 @@
             pltpu.VMEM((store_region.shape[0] // LANES, LANES), i32),
             pltpu.VMEM((date_flag.shape[0] // LANES, LANES), i32),
             pltpu.VMEM((devices, round_up(item_rows, 16), LANES), bf16),
-            pltpu.VMEM(((devices + 31) // 32 * item_rows, LANES), i32),
-            pltpu.VMEM(facts, f32), pltpu.VMEM((2, chunk, LANES), f32),
+            pltpu.VMEM((2, 16, LANES), i32),
+            pltpu.VMEM(facts, f32),
             pltpu.VMEM(facts, f32), pltpu.VMEM(facts, f32), pltpu.VMEM(facts, f32), pltpu.VMEM(facts, f32),
             pltpu.VMEM(facts, i32), pltpu.VMEM(facts, i32), pltpu.VMEM(facts, i32),
-            pltpu.VMEM((half * LANES, weeks // rep_size), bf16),
+            pltpu.VMEM(facts, i32),
+            pltpu.VMEM((prebuilt, rep_size * AGGS * regions, chunk * LANES), bf16),
             pltpu.VMEM((rep_size * AGGS * regions, weeks // rep_size), f32),
             pltpu.VMEM((rep_size, AGGS * regions, weeks // rep_size), bf16),
             pltpu.VMEM((devices, tile, weeks // rep_size), bf16),

time: 37.7 us -> 39.6 us (1.050)
  Pallas kernels: 35.4 us -> 37.3 us
    pallas_call x1, Pallas kernels: 35.4 us -> 37.3 us  [per_device(): pl.pallas_call(functools.partial(kernel, dom_size, rep_size, regions, ite...]
where the time goes in v3:
time: 39.6 us; the launch traced here: 39.4 us
  Pallas kernels  37.3 us (94%)
  local copies, waits for them, and re-layouts  1.42 us (4%)
  between operations  0.66 us (2%)
    pallas_call x1, Pallas kernels, per_device(): pl.pallas_call(functools.partial(kernel, dom_size, rep_size, regions, ite...  37.3 us
    unnamed x1, local copies, waits for them, and re-layouts  1.42 us

profile of v3, /device:TPU:0, one launch (start us, length us, event | category | flops | bytes accessed | tf_op | source)
XLA Modules:
  0.0 39.4 jit_solution(3699592490307867040)
XLA Ops:
  0.7 37.3 %shard_map.82 = f32[6,16,128]{2,1,0:T(8,128)} custom-call(s32[1]{0:T(128)S(6)} %copy.10.count_ref, s32[256,128]{1,0:T(8,128)} %date_hbm.1, s32[256,128]{1,0:T(8,128)} %item_hbm.1, s32[256,128]{1,0:T(8,128)} %store_hbm.1, f32[1024,128]{1,0:T(8,128)} %bitcast.6, f32[56,128]{1,0:T(8,128)} %bitcast.7, s32[1,128]{1,0:T(1,128)} %bitcast.9, s32[14,128]{1,0:T(8,128)} %bitcast.8), custom_call_target="tpu_custom_call" | custom-call | flops 805306368 | bytes 458752 | tf_op jit(solution)/shard_map/pallas_call | solution.py:388
  37.9 1.4 %copy.11 = f32[3,32,128]{2,1,0:T(8,128)} copy(f32[3,32,128]{2,1,0:T(8,128)} %bitcast.5) | data formatting | bytes 98304

commit v4 on v2

--- a/solution.py
+++ b/solution.py
@@ -376,7 +376,7 @@
     bf16, f32, i32 = jnp.bfloat16, jnp.float32, jnp.int32
     dma = pltpu.SemaphoreType.DMA
     vmem = pl.BlockSpec(memory_space=pltpu.VMEM)
-    hbm = pl.BlockSpec(memory_space=pl.ANY)
+    hbm = pl.BlockSpec(memory_space=pltpu.HBM)
     facts = (half, LANES)
     out = pl.pallas_call(
         functools.partial(kernel, dom_size, rep_size, regions, item_rows, slots, chunk),
@@ -407,7 +407,7 @@
             dma((dom_size,)), dma((tiles,)),
         ],
         compiler_params=pltpu.CompilerParams(
-            collective_id=0, has_side_effects=True, vmem_limit_bytes=60 * 1024 * 1024
+            collective_id=0, has_side_effects=True, vmem_limit_bytes=40 * 1024 * 1024
         ),
         cost_estimate=pl.CostEstimate(
             flops=2 * AGGS * regions * weeks * half * LANES, bytes_accessed=half * LANES * 28, transcendentals=0

time: 37.7 us -> 41.8 us (1.11)
  local copies, waits for them, and re-layouts: 1.42 us -> 5.77 us
    unnamed x1 -> x15, local copies, waits for them, and re-layouts: 1.42 us -> 5.77 us
where the time goes in v4:
time: 41.8 us; the launch traced here: 41.5 us
  Pallas kernels  35 us (84%)
  local copies, waits for them, and re-layouts  5.77 us (14%)
  between operations  0.69 us (2%)
    pallas_call x1, Pallas kernels, per_device(): pl.pallas_call(functools.partial(kernel, dom_size, rep_size, regions, ite...  35 us
    unnamed x15, local copies, waits for them, and re-layouts  5.77 us

profile of v4, /device:TPU:0, one launch (start us, length us, event | category | flops | bytes accessed | tf_op | source)
XLA Modules:
  0.0 41.5 jit_solution(18293033577538791050)
XLA Ops:
  0.0 0.0 copy-start.5
  0.7 0.0 copy-start.6
  0.7 0.0 copy-done.5
  0.7 0.6 %copy-done.6 = s32[128]{0:T(128)S(1)} copy-done((s32[128]{0:T(128)S(1)}, s32[128]{0:T(128)}, u32[]{:S(2)}) %copy-start.6) | copy-done | bytes 536
  1.3 0.0 copy-start
  1.3 1.0 %copy-done = f32[256,4,128]{2,1,0:T(4,128)S(1)} copy-done((f32[256,4,128]{2,1,0:T(4,128)S(1)}, f32[256,4,128]{2,1,0:T(4,128)}, u32[]{:S(2)}) %copy-start) | copy-done | bytes 524312
  2.4 0.0 copy-start.1
  2.4 0.9 %copy-done.1 = s32[256,128]{1,0:T(8,128)S(1)} copy-done((s32[256,128]{1,0:T(8,128)S(1)}, s32[256,128]{1,0:T(8,128)}, u32[]{:S(2)}) %copy-start.1) | copy-done | bytes 131096
  3.3 0.0 copy-start.2
  3.3 0.9 %copy-done.2 = s32[256,128]{1,0:T(8,128)S(1)} copy-done((s32[256,128]{1,0:T(8,128)S(1)}, s32[256,128]{1,0:T(8,128)}, u32[]{:S(2)}) %copy-start.2) | copy-done | bytes 131096
  4.2 0.0 copy-start.3
  4.2 0.9 %copy-done.3 = s32[256,128]{1,0:T(8,128)S(1)} copy-done((s32[256,128]{1,0:T(8,128)S(1)}, s32[256,128]{1,0:T(8,128)}, u32[]{:S(2)}) %copy-start.3) | copy-done | bytes 131096
  5.1 0.0 copy-start.4
  5.1 0.7 %copy-done.4 = f32[7168]{0:T(1024)S(1)} copy-done((f32[7168]{0:T(1024)S(1)}, f32[7168]{0:T(1024)}, u32[]{:S(2)}) %copy-start.4) | copy-done | bytes 28696
  5.8 35.0 %shard_map.82 = f32[6,16,128]{2,1,0:T(8,128)S(1)} custom-call(s32[1]{0:T(128)S(6)} %copy.10.count_ref, s32[256,128]{1,0:T(8,128)S(1)} %copy-done.1, s32[256,128]{1,0:T(8,128)S(1)} %copy-done.2, s32[256,128]{1,0:T(8,128)S(1)} %copy-done.3, f32[1024,128]{1,0:T(8,128)S(1)} %bitcast.6, f32[56,128]{1,0:T(8,128)S(1)} %bitcast.7, s32[1,128]{1,0:T(1,128)S(1)} %bitcast.9, ...), custom_call_target="tpu_custom_call" | custom-call | flops 805306368 | bytes 458752 | tf_op jit(solution)/shard_map/pallas_call | solution.py:381
  40.9 0.6 %copy.11 = f32[3,32,128]{2,1,0:T(8,128)} copy(f32[3,32,128]{2,1,0:T(8,128)S(1)} %bitcast.5) | data formatting | bytes 98304
Async XLA Ops:
  0.0 0.7 %copy-start.5 = (s32[1792]{0:T(1024)S(1)}, s32[1792]{0:T(1024)}, u32[]{:S(2)}) copy-start(s32[1792]{0:T(1024)} %param.15) | copy-start | bytes 21508
  0.7 0.7 %copy-start.6 = (s32[128]{0:T(128)S(1)}, s32[128]{0:T(128)}, u32[]{:S(2)}) copy-start(s32[128]{0:T(128)} %param.14) | copy-start | bytes 1540
  1.3 1.0 %copy-start = (f32[256,4,128]{2,1,0:T(4,128)S(1)}, f32[256,4,128]{2,1,0:T(4,128)}, u32[]{:S(2)}) copy-start(f32[256,4,128]{2,1,0:T(4,128)} %param.11) | copy-start | bytes 1572868
  2.4 0.9 %copy-start.1 = (s32[256,128]{1,0:T(8,128)S(1)}, s32[256,128]{1,0:T(8,128)}, u32[]{:S(2)}) copy-start(s32[256,128]{1,0:T(8,128)} %date_hbm.1) | copy-start | bytes 393220
  3.3 0.9 %copy-start.2 = (s32[256,128]{1,0:T(8,128)S(1)}, s32[256,128]{1,0:T(8,128)}, u32[]{:S(2)}) copy-start(s32[256,128]{1,0:T(8,128)} %item_hbm.1) | copy-start | bytes 393220
  4.2 0.9 %copy-start.3 = (s32[256,128]{1,0:T(8,128)S(1)}, s32[256,128]{1,0:T(8,128)}, u32[]{:S(2)}) copy-start(s32[256,128]{1,0:T(8,128)} %store_hbm.1) | copy-start | bytes 393220
  5.1 0.7 %copy-start.4 = (f32[7168]{0:T(1024)S(1)}, f32[7168]{0:T(1024)}, u32[]{:S(2)}) copy-start(f32[7168]{0:T(1024)} %param.13) | copy-start | bytes 86020
